TPU v7x, 32 devices: a whole 2x2x4 slice. The times are simulated.
32 devices in a mesh: row: 16 (over z, x, core), col: 2 (over y).
Axes of the slice: x: 2, y: 2, z: 4, core: 2. Of those that a mesh axis runs over, the one named last changes fastest.
Arguments:
- trail_adjoint: float32 [16, 128, 2, 1024], P('row', None, 'col'), may hold values from -2.8 to 2.8, as said below
- panel_one: float32 [2048, 512], P(('row', 'col')), may hold values from -0.125 to 0.125
- panel_two: float32 [2048, 512], P(('row', 'col')), may hold values from -0.125 to 0.125
- upstream_one: float32 [2048, 512], P(('row', 'col')), may hold values from -6 to 6
- upstream_two: float32 [2048, 512], P(('row', 'col')), may hold values from -6 to 6
- pivot_one: float32 [512, 512], replicated, may hold values from -1 to 2, as said below
- pivot_two: float32 [512, 512], replicated, may hold values from -1 to 2, as said below
- link_block: float32 [512, 512], replicated, may hold values from -0.25 to 0.25
- pivot_adjoint: float32 [2, 512, 512], replicated, may hold values from -6 to 6
Outputs:
- strip_grad_one: float32 [2048, 512], P(('row', 'col'))
- strip_grad_two: float32 [2048, 512], P(('row', 'col'))
- block_grads: float32 [3, 512, 512], replicated
Inputs may be any that keep to these rules, and one draw needn't show every extreme that they name: trail_adjoint[a, c * 64 + s, c2, a2 * 64 + s2] equals trail_adjoint[a2, c2 * 64 + s2, c, a * 64 + s], so sbar is symmetric. `pivot_one`: lower triangular, diagonal entries between 1 and 2. `pivot_two`: lower triangular, diagonal entries between 1 and 2.
All inputs are finite; a program needn't handle non-finite values.
Results may differ from a plain program's by a relative error of at most 0.000062.
Values sent between devices are 32-bit elements; how exact they have to be, the bound alone decides.
A program may use at most 128 MiB of HBM per device.

v0:
```python
import jax
import jax.numpy as jnp
from jax import lax
from jax.sharding import PartitionSpec as P


def exact_dot(left, right):
    return jnp.dot(left, right, precision=lax.Precision.HIGHEST, preferred_element_type=jnp.float32)


def cross_dot(left, right):
    return lax.dot_general(
        left,
        right,
        (((0,), (0,)), ((), ())),
        precision=lax.Precision.HIGHEST,
        preferred_element_type=jnp.float32,
    )


def lower_inverse(factor):
    identity = jnp.eye(factor.shape[0], dtype=jnp.float32)
    return jax.scipy.linalg.solve_triangular(factor, identity, lower=True)


def chol_grad(factor, cotangent, inverse):
    product = cross_dot(factor, jnp.tril(cotangent))
    halved = jnp.tril(product) - 0.5 * jnp.diag(jnp.diag(product))
    inner = cross_dot(inverse, exact_dot(halved, inverse))
    return 0.5 * (inner + inner.T)


def local(
    trail_adjoint,
    panel_one,
    panel_two,
    upstream_one,
    upstream_two,
    pivot_one,
    pivot_two,
    link_block,
    pivot_adjoint,
):
    width = panel_one.shape[1]
    stacked = jnp.concatenate([panel_one, panel_two], axis=1)
    matrix = trail_adjoint.reshape(trail_adjoint.shape[1], trail_adjoint.shape[3])
    summed = exact_dot(matrix, lax.all_gather(stacked, "row", axis=0, tiled=True))
    carried = lax.psum_scatter(2.0 * summed, "col", scatter_dimension=0, tiled=True)
    pressed_one = upstream_one - carried[:, :width]
    pressed_two = upstream_two - carried[:, width:]
    inverse_one = lower_inverse(pivot_one)
    inverse_two = lower_inverse(pivot_two)
    grad_two = exact_dot(pressed_two, inverse_two)
    cross_two, cross_link = lax.psum(
        (cross_dot(grad_two, panel_two), cross_dot(grad_two, panel_one)), ("row", "col")
    )
    grad_one = exact_dot(pressed_one - exact_dot(grad_two, link_block), inverse_one)
    cross_one = lax.psum(cross_dot(grad_one, panel_one), ("row", "col"))
    pivot_grad_two = chol_grad(pivot_two, pivot_adjoint[1] - cross_two, inverse_two)
    link_grad = -cross_link - 2.0 * exact_dot(pivot_grad_two, link_block)
    link_input = exact_dot(link_grad, inverse_one)
    pivot_grad_one = chol_grad(
        pivot_one, pivot_adjoint[0] - cross_dot(link_input, link_block) - cross_one, inverse_one
    )
    return (grad_one, grad_two, jnp.stack([pivot_grad_one, link_input, pivot_grad_two]))


def solution(mesh):
    return jax.shard_map(
        local,
        mesh=mesh,
        in_specs=(
            P("row", None, "col", None),
            P(("row", "col"), None),
            P(("row", "col"), None),
            P(("row", "col"), None),
            P(("row", "col"), None),
            P(),
            P(),
            P(),
            P(),
        ),
        out_specs=(P(("row", "col"), None), P(("row", "col"), None), P()),
        check_vma=False,
    )
```

profile of v0, /device:TPU:1, one launch (start us, length us, event | category | flops | bytes accessed | tf_op | source)
XLA Modules:
  0.0 357.7 jit_solution(7668951529839288907)
XLA Ops:
  7.2 1.8 pad_maximum_fusion.3
  9.2 1.3 fusion.11
  10.5 7.9 %while.5 = (s32[]{:T(128)}, f32[512,512]{1,0:T(8,128)S(1)}, s32[4,2]{0,1:T(2,128)S(1)}, f32[4,128,128]{2,1,0:T(8,128)S(1)}, s32[]{:T(128)}) while((s32[]{:T(128)}, f32[512,512]{1,0:T(8,128)S(1)}, s32[4,2]{0,1:T(2,128)S(1)}, f32[4,128,128]{2,1,0:T(8,128)S(1)}, s32[]{:T(128)}) %tuple.45), condition=%wide.while_cond.clone, body=%wide.while_body.clone.sunk | while | flops 2 | bytes 131181 | solution.py:23
  10.6 0.5 fusion.122
  11.2 1.4 bitcast_dynamic-update-slice_fusion.5
  12.6 0.5 fusion.122
  13.1 1.4 bitcast_dynamic-update-slice_fusion.5
  14.6 0.5 fusion.122
  15.1 1.4 bitcast_dynamic-update-slice_fusion.5
  16.6 0.5 fusion.122
  17.1 1.4 bitcast_dynamic-update-slice_fusion.5
  18.5 39.9 %custom-call.9 = f32[4,128,128]{1,2,0:T(8,128)} custom-call(f32[4,128,128]{2,1,0:T(8,128)S(1)} %get-tuple-element.19), custom_call_target="InvertDiagBlocksLowerTriangular" | custom-call | tf_op jit(solution)/shard_map/jit(_solve_triangular)/triangular_solve | solution.py:23
  58.4 1.1 fusion.12
  59.6 11.6 %while.4 = (s32[]{:T(128)}, f32[512,512]{1,0:T(8,128)}, s32[4,2]{0,1:T(2,128)S(1)}, f32[4,128,128]{2,1,0:T(8,128)S(1)}, s32[]{:T(128)}) while((s32[]{:T(128)}, f32[512,512]{1,0:T(8,128)}, s32[4,2]{0,1:T(2,128)S(1)}, f32[4,128,128]{2,1,0:T(8,128)S(1)}, s32[]{:T(128)}) %tuple.55), condition=%wide.while_cond, body=%wide.while_body.sunk | while | flops 2 | bytes 131181 | solution.py:23
  59.7 0.5 fusion.121
  60.2 2.3 bitcast_dynamic-update-slice_fusion.4
  62.6 0.5 fusion.121
  63.1 2.3 bitcast_dynamic-update-slice_fusion.4
  65.5 0.5 fusion.121
  66.0 2.3 bitcast_dynamic-update-slice_fusion.4
  68.4 0.5 fusion.121
  68.9 2.2 bitcast_dynamic-update-slice_fusion.4
  71.2 40.4 %custom-call.8 = f32[4,128,128]{1,2,0:T(8,128)} custom-call(f32[4,128,128]{2,1,0:T(8,128)S(1)} %get-tuple-element.18), custom_call_target="InvertDiagBlocksLowerTriangular" | custom-call | tf_op jit(solution)/shard_map/jit(_solve_triangular)/triangular_solve | solution.py:23
  111.7 1.3 fusion.54
  113.4 1.3 fusion.66
  114.7 1.4 convolution_subtract_fusion.1
  116.1 1.3 fusion.64
  117.4 1.7 convolution_subtract_fusion.5
  119.0 2.0 fusion.63
  121.0 1.3 fusion.56
  122.3 1.9 convolution_subtract_fusion.4
  124.2 9.8 %fusion.3 = f32[128,1024]{0,1:T(8,128)} fusion(f32[1024,1024]{1,0:T(8,128)} %all-gather.2.cloned.1.call-done, f32[1,128,1,1024]{3,2,1,0:T(1,128)} %param.11), kind=kOutput, calls=%fused_computation.15 | convolution fusion | flops 1610743808 | bytes 5242880 | tf_op jit(solution)/shard_map/dot_general | solution.py:8
  134.0 2.0 copy.44
  136.3 1.4 fusion.70
  137.7 0.9 copy.37
  138.5 1.3 convolution_subtract_fusion.3
  139.9 1.3 fusion.68
  141.2 1.7 convolution_subtract_fusion.6
  142.8 1.3 fusion.67
  144.2 8.7 %reduce-scatter.4.cloned.1.call-done = f32[64,1024]{1,0:T(8,128)} async-done(((f32[128,1024]{1,0:T(8,128)}), f32[64,1024]{1,0:T(8,128)}) %reduce-scatter.4.cloned.1.call-update) | async-done | bytes 262160 | tf_op jit(solution)/shard_map/reduce_scatter | solution.py:48
  152.8 1.0 slice.56
  153.8 0.8 copy.47
  154.7 1.8 fusion.52
  156.5 3.0 fusion.89
  159.5 2.9 fusion.90
  162.4 0.8 convolution_subtract_fusion.7
  163.2 0.8 fusion.86
  164.0 2.1 fusion.91
  166.1 137.6 %all-reduce.3.cloned.1.call-done = (f32[512,512]{1,0:T(8,128)}, f32[512,512]{1,0:T(8,128)}, f32[512,512]{1,0:T(8,128)}) async-done(((f32[512,512]{1,0:T(8,128)}, f32[512,512]{1,0:T(8,128)}, f32[512,512]{1,0:T(8,128)}), (f32[512,512]{1,0:T(8,128)}, f32[512,512]{1,0:T(8,128)}, f32[512,512]{1,0:T(8,128)})) %all-reduce.3.cloned.1.call-update) | async-done | bytes 3145744 | tf_op jit(solution)/shard_map/psum | solution.py:54
  303.7 3.8 %convolution_bitcast_fusion.1 = f32[512,512]{1,0:T(8,128)S(1)} fusion(f32[512,512]{1,0:T(8,128)} %param.17, f32[512,512]{1,0:T(8,128)} %get-tuple-element.42, f32[2,512,512]{2,1,0:T(8,128)} %param.19), kind=kOutput, calls=%fused_computation.12 | convolution fusion | flops 1611399168 | bytes 4194304 | tf_op jit(solution)/shard_map/dot_general | solution.py:12
  307.5 4.7 %gather_fusion = f32[512]{0:T(512)S(1)} fusion(f32[512,512]{1,0:T(8,128)S(1)} %convolution_bitcast_fusion.1, s32[512]{0:T(512)S(1)} %bitcast.107), kind=kCustom, calls=%fused_computation | custom fusion | bytes 8192 | tf_op jit(solution)/shard_map/jit(_diag)/jit(diagonal)/cond/branch_0_fun/gather | solution.py:28
  312.3 2.9 fusion.14
  315.2 1.9 fusion.60
  317.4 0.9 copy-done.1
  318.4 3.3 fusion.1
  321.8 1.9 fusion.85
  323.7 1.9 fusion.2
  325.6 2.9 convolution_bitcast_fusion
  328.5 9.3 %gather_fusion.1 = f32[512]{0:T(512)S(1)} fusion(f32[512,512]{1,0:T(8,128)} %convolution_bitcast_fusion, s32[512]{0:T(512)S(1)} %bitcast.108), kind=kCustom, calls=%fused_computation.1 | custom fusion | bytes 8192 | tf_op jit(solution)/shard_map/jit(_diag)/jit(diagonal)/cond/branch_0_fun/gather | solution.py:28
  337.8 3.4 fusion.17
  341.2 2.9 fusion.84
  344.1 2.5 copy.41
  346.6 2.4 fusion.5
  349.0 2.0 pad_maximum_fusion
  (74 shorter events, 1.9 us)
Async XLA Ops:
  7.2 155.3 %copy-start = (f32[512,512]{1,0:T(8,128)S(1)}, f32[512,512]{1,0:T(8,128)}, u32[]{:S(2)}) copy-start(f32[512,512]{1,0:T(8,128)} %param.18) | copy-start | bytes 3145732
  7.2 51.3 %copy-start.9 = (f32[512,512]{1,0:T(8,128)S(1)}, f32[512,512]{1,0:T(8,128)}, u32[]{:S(2)}) copy-start(f32[512,512]{1,0:T(8,128)} %param.17) | copy-start | bytes 3145732
  7.2 117.0 %all-gather.2.cloned.1.call-start = ((), (), s32[]{:S(2)}) async-start(), calls=%async_computation.1 | async-start | bytes 4456448 | tf_op jit(solution)/shard_map/all_gather | solution.py:47
  9.1 143.7 %reduce-scatter.4.cloned.1.call-start = ((), (), s32[]{:S(2)}) async-start(), calls=%async_computation.2 | async-start | bytes 786432 | tf_op jit(solution)/shard_map/reduce_scatter | solution.py:48
  18.5 94.5 %copy-start.10 = (f32[512,512]{1,0:T(8,128)}, f32[512,512]{1,0:T(8,128)S(1)}, u32[]{:S(2)}) copy-start(f32[512,512]{1,0:T(8,128)S(1)} %get-tuple-element.152) | copy-start | bytes 3145732
  114.7 48.5 %copy-start.2 = (f32[128,512]{1,0:T(8,128)}, f32[128,512]{1,0:T(8,128)S(1)}, u32[]{:S(2)}) copy-start(f32[128,512]{1,0:T(8,128)S(1)} %fusion.66) | copy-start | bytes 786436
  117.4 45.8 %copy-start.6 = (f32[128,512]{1,0:T(8,128)}, f32[128,512]{1,0:T(8,128)S(1)}, u32[]{:S(2)}) copy-start(f32[128,512]{1,0:T(8,128)S(1)} %fusion.64) | copy-start | bytes 786436
  124.2 13.5 %copy-start.23 = (f32[64,512]{1,0:T(8,128)S(1)}, f32[64,512]{1,0:T(8,128)}, u32[]{:S(2)}) copy-start(f32[64,512]{1,0:T(8,128)} %param.15) | copy-start | bytes 393220
  136.0 167.7 %all-reduce.3.cloned.1.call-start = ((), (), s32[]{:S(2)}) async-start(), calls=%async_computation.3 | async-start | bytes 6291456 | tf_op jit(solution)/shard_map/psum | solution.py:54
  141.1 1.7 copy-start.14
  142.8 19.6 %copy-start.24 = (f32[64,512]{1,0:T(8,128)S(1)}, f32[64,512]{1,0:T(8,128)}, u32[]{:S(2)}) copy-start(f32[64,512]{1,0:T(8,128)} %param.14) | copy-start | bytes 393220
  144.1 10.5 %copy-start.20 = (f32[128,512]{1,0:T(8,128)}, f32[128,512]{1,0:T(8,128)S(1)}, u32[]{:S(2)}) copy-start(f32[128,512]{1,0:T(8,128)S(1)} %fusion.67) | copy-start | bytes 786436
  152.8 9.6 %copy-start.22 = (f32[64,1024]{1,0:T(8,128)S(1)}, f32[64,1024]{1,0:T(8,128)}, u32[]{:S(2)}) copy-start(f32[64,1024]{1,0:T(8,128)} %reduce-scatter.4.cloned.1.call-done) | copy-start | bytes 786436
  153.8 9.4 %copy-start.11 = (f32[128,512]{1,0:T(8,128)S(1)}, f32[128,512]{1,0:T(8,128)}, u32[]{:S(2)}) copy-start(f32[128,512]{1,0:T(8,128)} %fusion.63) | copy-start | bytes 786436
  156.5 9.5 %copy-start.17 = (f32[64,512]{1,0:T(8,128)}, f32[64,512]{1,0:T(8,128)S(1)}, u32[]{:S(2)}) copy-start(f32[64,512]{1,0:T(8,128)S(1)} %fusion.52) | copy-start | bytes 393220
  156.5 7.5 %copy-start.18 = (f32[64,512]{1,0:T(8,128)S(1)}, f32[64,512]{1,0:T(8,128)}, u32[]{:S(2)}) copy-start(f32[64,512]{1,0:T(8,128)} %param.12) | copy-start | bytes 393220
  164.0 139.7 %copy-start.25 = (f32[64,512]{1,0:T(8,128)}, f32[64,512]{1,0:T(8,128)S(1)}, u32[]{:S(2)}) copy-start(f32[64,512]{1,0:T(8,128)S(1)} %fusion.86) | copy-start | bytes 393220
  303.7 8.5 %copy-start.15 = (f32[128,512]{1,0:T(8,128)S(1)}, f32[128,512]{1,0:T(8,128)}, u32[]{:S(2)}) copy-start(f32[128,512]{1,0:T(8,128)} %copy-done.14) | copy-start | bytes 786436
  312.3 2.9 copy-start.21
  317.4 1.0 copy-start.1
  317.4 4.3 %copy-start.3 = (f32[128,512]{1,0:T(8,128)S(1)}, f32[128,512]{1,0:T(8,128)}, u32[]{:S(2)}) copy-start(f32[128,512]{1,0:T(8,128)} %copy-done.2) | copy-start | bytes 786436
  317.4 4.3 %copy-start.7 = (f32[128,512]{1,0:T(8,128)S(1)}, f32[128,512]{1,0:T(8,128)}, u32[]{:S(2)}) copy-start(f32[128,512]{1,0:T(8,128)} %copy-done.6) | copy-start | bytes 786436
  317.4 4.3 %copy-start.12 = (f32[128,512]{1,0:T(8,128)S(1)}, f32[128,512]{1,0:T(8,128)}, u32[]{:S(2)}) copy-start(f32[128,512]{1,0:T(8,128)} %fusion.63) | copy-start | bytes 786436
  318.4 5.2 %copy-start.16 = (f32[2,512,512]{2,1,0:T(8,128)S(1)}, f32[2,512,512]{2,1,0:T(8,128)}, u32[]{:S(2)}) copy-start(f32[2,512,512]{2,1,0:T(8,128)} %param.19) | copy-start | bytes 6291460
  318.4 5.3 %copy-start.19 = (f32[512,512]{1,0:T(8,128)S(1)}, f32[512,512]{1,0:T(8,128)}, u32[]{:S(2)}) copy-start(f32[512,512]{1,0:T(8,128)} %get-tuple-element.44) | copy-start | bytes 3145732
  323.6 2.0 copy-start.5
  337.8 3.4 copy-start.4
  337.8 3.4 copy-start.8
  337.8 3.4 copy-start.13
Sparse Core Ops, SparseCore 0:
  10.2 54.2 all-gather.1
  136.2 16.6 reduce-scatter.3
  166.2 137.4 all-reduce.2
where the time goes:
time: 365 us; the launch traced here: 358 us
  waiting for transfers between devices  146 us (40%)
  other arithmetic  89.1 us (24%)
  matrix products  65.2 us (18%)
  local copies, waits for them, and re-layouts  42.1 us (12%)
  between operations  14.6 us (4%)
    psum x1, waiting for transfers between devices, local(): lax.psum((cross_dot(grad_two, panel_two), cross_dot(grad_two, panel_one))...  138 us
    another operation x5, other arithmetic, lower_inverse(): return jax.scipy.linalg.solve_triangular(factor, identity, lower=True)  82.8 us
    dot_general x8, matrix products, exact_dot(): jnp.dot(left, right, precision=lax.Precision.HIGHEST, preferred_element_t...  24.6 us
    dot_general x8, matrix products, cross_dot(): lax.dot_general(left, right, (((0,), (0,)), ((), ())), precision=lax.Prec...  21.3 us
    another operation x27, local copies, waits for them, and re-layouts, lower_inverse(): return jax.scipy.linalg.solve_triangular(factor, identity, lower=True)  19.4 us
    another operation x14, matrix products, lower_inverse(): return jax.scipy.linalg.solve_triangular(factor, identity, lower=True)  19.3 us
    gather x2, local copies, waits for them, and re-layouts, chol_grad(): halved = jnp.tril(product) - 0.5 * jnp.diag(jnp.diag(product))  14 us
    reduce_scatter x1, waiting for transfers between devices, local(): lax.psum_scatter(2.0 * summed, 'col', scatter_dimension=0, tiled=True)  8.68 us
  transfers between devices with their start and end apart: 3, of which 2 were waited for; matrix products, arithmetic and copies ran while one was open for 34% of the time, Pallas kernels for 0%

commit v1 on v0

v1 whole, which is shorter than its diff:
```python
import jax
import jax.numpy as jnp
from jax import lax
from jax.experimental import pallas as pl
from jax.experimental.pallas import tpu as pltpu
from jax.sharding import PartitionSpec as P

TILE = 128
BASE = 8


def dot(left, right, precision=lax.Precision.HIGHEST):
    return jnp.dot(left, right, precision=precision, preferred_element_type=jnp.float32)


def high(left, right):
    return dot(left, right, lax.Precision.HIGH)


def tile_inverses(tiles):
    size = tiles[0].shape[0]
    row = lax.broadcasted_iota(jnp.int32, (size, size), 0)
    col = lax.broadcasted_iota(jnp.int32, (size, size), 1)
    eye = row == col
    one = jnp.where(eye, 1.0, 0.0)
    base = (row // BASE == col // BASE) & (row > col)
    nil, across = [], []
    for tile in tiles:
        diag = jnp.where(eye, tile, 0.0)
        down = 1.0 / jnp.sum(diag, axis=1, keepdims=True)
        across.append(1.0 / jnp.sum(diag, axis=0, keepdims=True))
        nil.append(jnp.where(base, -tile * down, 0.0))
    found = [one + n for n in nil]
    power = nil
    reach = 2
    while reach < BASE:
        power = [dot(p, p) for p in power]
        found = [f + dot(f, p) for f, p in zip(found, power)]
        reach *= 2
    found = [f * a for f, a in zip(found, across)]
    step = BASE
    while step < size:
        level = (row // (2 * step) == col // (2 * step)) & (row // step != col // step) & (row > col)
        below = [dot(jnp.where(level, t, 0.0), f) for t, f in zip(tiles, found)]
        found = [f - dot(f, b) for f, b in zip(found, below)]
        step *= 2
    return found


def invert(factors, outs):
    width = factors[0].shape[0]
    count = width // TILE
    tiles = [f[pl.ds(t * TILE, TILE), pl.ds(t * TILE, TILE)] for f in factors for t in range(count)]
    found = tile_inverses(tiles)
    for i, out in enumerate(outs):
        out[...] = jnp.zeros_like(out)
        for t in range(count):
            out[pl.ds(t * TILE, TILE), pl.ds(t * TILE, TILE)] = found[i * count + t]
    step = TILE
    while step < width:
        for at in range(0, width, 2 * step):
            top, low = pl.ds(at, step), pl.ds(at + step, step)
            belows = [dot(f[low, top], o[top, top]) for f, o in zip(factors, outs)]
            for o, b in zip(outs, belows):
                o[low, top] = -dot(o[low, low], b)
        step *= 2


def prepare(one_ref, two_ref, link_ref, adj_ref, inv_one, inv_two, inv_one_t, inv_two_t, mixed, mixed_t, adj_one, adj_two):
    invert((one_ref, two_ref), (inv_one, inv_two))
    inv_one_t[...] = inv_one[...].T
    inv_two_t[...] = inv_two[...].T
    mixed[...] = high(inv_two[...], link_ref[...])
    mixed_t[...] = mixed[...].T
    adj_one[...] = high(one_ref[...].T, adj_ref[0])
    adj_two[...] = high(two_ref[...].T, adj_ref[1])


def half_symmetric(x):
    row = lax.broadcasted_iota(jnp.int32, x.shape, 0)
    col = lax.broadcasted_iota(jnp.int32, x.shape, 1)
    return 0.5 * (jnp.where(row > col, x, 0.0) + jnp.where(row >= col, x, 0.0).T)


def finish(sums, inv_one, inv_two, inv_one_t, inv_two_t, mixed, mixed_t, adj_one, adj_two, out):
    sym_two = half_symmetric(adj_two[...] - sums[2])
    out[2] = high(inv_two_t[...], high(sym_two, inv_two[...]))
    turned = high(sym_two, mixed[...])
    out[1] = high(high(-inv_two_t[...], sums[1] + 2.0 * turned), inv_one[...])
    cross = high(mixed_t[...], sums[1] + turned)
    sym_one = half_symmetric(adj_one[...] - sums[0]) + 0.5 * (cross + cross.T)
    out[0] = high(inv_one_t[...], high(sym_one, inv_one[...]))


def whole(count):
    return [pl.BlockSpec(memory_space=pltpu.VMEM)] * count


def local(
    trail_adjoint,
    panel_one,
    panel_two,
    upstream_one,
    upstream_two,
    pivot_one,
    pivot_two,
    link_block,
    pivot_adjoint,
):
    width = panel_one.shape[1]
    square = jax.ShapeDtypeStruct((width, width), jnp.float32)
    params = pltpu.CompilerParams(vmem_limit_bytes=48 << 20)
    cost = pl.CostEstimate(flops=16 * width**3, bytes_accessed=48 * width**2, transcendentals=0)
    prepared = pl.pallas_call(
        prepare,
        out_shape=[square] * 8,
        in_specs=whole(4),
        out_specs=whole(8),
        compiler_params=params,
        cost_estimate=cost,
        name="prepare",
    )(pivot_one, pivot_two, link_block, pivot_adjoint)
    inverse_one, inverse_two = prepared[:2]
    stacked = jnp.concatenate([panel_one, panel_two], axis=1)
    matrix = trail_adjoint.reshape(trail_adjoint.shape[1], trail_adjoint.shape[3])
    summed = high(matrix, lax.all_gather(stacked, "row", axis=0, tiled=True))
    carried = lax.psum_scatter(2.0 * summed, "col", scatter_dimension=0, tiled=True)
    pressed_one = upstream_one - carried[:, :width]
    pressed_two = upstream_two - carried[:, width:]
    sums = lax.psum(
        jnp.stack(
            [
                high(pressed_one.T, panel_one),
                high(pressed_two.T, panel_one),
                high(pressed_two.T, panel_two),
            ]
        ),
        ("row", "col"),
    )
    grad_two = high(pressed_two, inverse_two)
    grad_one = high(pressed_one - high(grad_two, link_block), inverse_one)
    grads = pl.pallas_call(
        finish,
        out_shape=jax.ShapeDtypeStruct((3, width, width), jnp.float32),
        in_specs=whole(9),
        out_specs=pl.BlockSpec(memory_space=pltpu.VMEM),
        compiler_params=params,
        cost_estimate=cost,
        name="finish",
    )(sums, *prepared)
    return grad_one, grad_two, grads


def solution(mesh):
    return jax.shard_map(
        local,
        mesh=mesh,
        in_specs=(
            P("row", None, "col", None),
            P(("row", "col"), None),
            P(("row", "col"), None),
            P(("row", "col"), None),
            P(("row", "col"), None),
            P(),
            P(),
            P(),
            P(),
        ),
        out_specs=(P(("row", "col"), None), P(("row", "col"), None), P()),
        check_vma=False,
    )
```

time: 365 us -> 250 us (0.68); the launches traced: 358 us -> 247 us
  other arithmetic: 89.1 us -> 3.66 us
  matrix products: 65.2 us -> 9.94 us
  waiting for transfers between devices: 146 us -> 186 us
  local copies, waits for them, and re-layouts: 42.1 us -> 7.01 us
  Pallas kernels: 0 us -> 26.2 us
    another operation x7 -> x1, other arithmetic: 87.1 us -> 1.97 us  [local(): jnp.stack([high(pressed_one.T, panel_one), high(pressed_two.T, panel_one)...]
    all_gather x1, waiting for transfers between devices: 0.01 us -> 54.8 us  [local(): summed = high(matrix, lax.all_gather(stacked, 'row', axis=0, tiled=True))]
    dot_general x16 -> x7, matrix products: 45.9 us -> 9.94 us  [dot(): jnp.dot(left, right, precision=precision, preferred_element_type=jnp.floa...]
    pallas_call x0 -> x2, Pallas kernels: none -> 26.2 us  [the longest x1 14.3 us: local(): pl.pallas_call(prepare, out_shape=[square] * 8, in_specs=whole(4), out_sp...]
    another operation x27 -> x0, local copies, waits for them, and re-layouts: 19.4 us -> none  [lower_inverse(): return jax.scipy.linalg.solve_triangular(factor, identity, lower=True)]
    another operation x14 -> x0, matrix products: 19.3 us -> none  [lower_inverse(): return jax.scipy.linalg.solve_triangular(factor, identity, lower=True)]
    psum x1, waiting for transfers between devices: 138 us -> 119 us  [local(): lax.psum(jnp.stack([high(pressed_one.T, panel_one), high(pressed_two.T, p...]
    gather x2 -> x0, local copies, waits for them, and re-layouts: 14 us -> none  [chol_grad(): halved = jnp.tril(product) - 0.5 * jnp.diag(jnp.diag(product))]
  transfers between devices with their start and end apart: 3 -> 3, of which waited for: 2 -> 3; matrix products, arithmetic and copies ran while one was open for 34% -> 1% of each run, Pallas kernels for 0% -> 6%
where the time goes in v1:
time: 250 us; the launch traced here: 247 us
  waiting for transfers between devices  186 us (74%)
  Pallas kernels  26.2 us (10%)
  between operations  14 us (6%)
  matrix products  9.94 us (4%)
  local copies, waits for them, and re-layouts  7.01 us (3%)
  other arithmetic  3.66 us (1%)
    psum x1, waiting for transfers between devices, local(): lax.psum(jnp.stack([high(pressed_one.T, panel_one), high(pressed_two.T, p...  119 us
    all_gather x1, waiting for transfers between devices, local(): summed = high(matrix, lax.all_gather(stacked, 'row', axis=0, tiled=True))  54.8 us
    pallas_call x1, Pallas kernels, local(): pl.pallas_call(prepare, out_shape=[square] * 8, in_specs=whole(4), out_sp...  14.3 us
    unnamed x4, waiting for transfers between devices  12.3 us
    pallas_call x1, Pallas kernels, local(): pl.pallas_call(finish, out_shape=jax.ShapeDtypeStruct((3, width, width),...  11.9 us
    dot_general x7, matrix products, dot(): jnp.dot(left, right, precision=precision, preferred_element_type=jnp.floa...  9.94 us
    unnamed x37, local copies, waits for them, and re-layouts  6.03 us
  transfers between devices with their start and end apart: 3, of which 3 were waited for; matrix products, arithmetic and copies ran while one was open for 1% of the time, Pallas kernels for 6%

profile of v1, /device:TPU:1, one launch (start us, length us, event | category | flops | bytes accessed | tf_op | source)
XLA Modules:
  0.0 247.4 jit_solution(17243715121019694629)
XLA Ops:
  7.2 0.0 all-gather.2.cloned.1.call-start
  7.2 1.7 pad_maximum_fusion.1
  8.9 0.0 all-gather.2.cloned.1.call-update
  8.9 0.0 copy-start.14
  8.9 0.0 copy-start.15
  8.9 0.0 copy-start.10
  9.0 0.0 reduce-scatter.4.cloned.1.call-start
  9.0 54.8 %all-gather.2.cloned.1.call-done = f32[1024,1024]{1,0:T(8,128)} async-done(((f32[64,1024]{1,0:T(8,128)}), f32[1024,1024]{1,0:T(8,128)}) %all-gather.2.cloned.1.call-update) | async-done | bytes 4194320 | tf_op jit(solution)/shard_map/all_gather | solution.py:126
  63.8 5.7 %fusion = f32[128,1024]{0,1:T(8,128)S(1)} fusion(f32[1024,1024]{1,0:T(8,128)} %all-gather.2.cloned.1.call-done, f32[1,128,1,1024]{3,2,1,0:T(1,128)} %param.9), kind=kOutput, calls=%fused_computation.5 | convolution fusion | flops 805437440 | bytes 5242880 | tf_op jit(solution)/shard_map/dot_general | solution.py:13
  69.6 0.0 copy-start.12
  69.6 1.0 copy.16
  70.6 0.0 reduce-scatter.4.cloned.1.call-update
  70.6 0.2 all-reduce.2.cloned.1.call-start
  70.8 0.0 copy-done.14
  70.8 0.1 copy.15
  71.0 0.0 copy-done.15
  71.0 0.1 copy.14
  71.1 0.0 copy-start.6
  71.1 12.3 %reduce-scatter.4.cloned.1.call-done = f32[64,1024]{1,0:T(8,128)} async-done(((f32[128,1024]{1,0:T(8,128)}), f32[64,1024]{1,0:T(8,128)}) %reduce-scatter.4.cloned.1.call-update) | async-done | bytes 262160
  83.4 1.0 fusion.8
  84.4 0.1 copy.20
  84.5 0.0 copy-done.10
  84.5 0.0 copy-start.4
  84.5 0.6 convolution_bitcast_fusion.1
  85.1 0.0 copy-done.12
  85.1 0.6 convolution_bitcast_fusion
  85.7 0.1 copy.19
  85.8 0.0 copy-start.8
  85.8 0.6 convolution_bitcast_fusion.2
  86.4 0.0 copy-done.6
  86.4 2.0 pad_maximum_fusion
  88.4 0.0 copy-done.4
  88.4 0.0 copy-done.8
  88.4 0.0 all-reduce.2.cloned.1.call-update
  88.4 0.0 copy-start.5
  88.4 0.0 copy-start.7
  88.4 0.0 copy-start.9
  88.4 0.0 copy-start.11
  88.4 14.3 %prepare.1 = (f32[512,512]{1,0:T(8,128)S(1)}, f32[512,512]{1,0:T(8,128)S(1)}, f32[512,512]{1,0:T(8,128)S(1)}, f32[512,512]{1,0:T(8,128)S(1)}, f32[512,512]{1,0:T...) custom-call(f32[512,512]{1,0:T(8,128)} %one_ref.1, f32[512,512]{1,0:T(8,128)} %two_ref.1, ...), custom_call_target="tpu_custom_call" | custom-call | flops 2147483648 | bytes 12582912 | tf_op jit(solution)/shard_map/prepare/pallas_call | solution.py:114
  102.8 0.0 copy-start
  102.8 1.0 copy-done
  103.7 0.0 copy-start.2
  103.7 1.1 copy-done.2
  104.8 0.0 copy-done.5
  104.8 0.4 fusion.6
  105.2 0.0 copy-done.7
  105.2 0.0 copy-done.9
  105.3 0.0 copy-done.11
  105.3 0.0 copy-start.13
  105.3 1.0 convolution_subtract_fusion
  106.3 1.1 fusion.9
  107.4 119.1 %all-reduce.2.cloned.1.call-done.sums = f32[3,512,512]{2,1,0:T(8,128)} async-done(((f32[3,512,512]{2,1,0:T(8,128)}), f32[3,512,512]{2,1,0:T(8,128)}) %all-reduce.2.cloned.1.call-update) | async-done | bytes 3145744 | tf_op jit(solution)/shard_map/psum | solution.py:130
  226.5 0.0 copy-start.1
  226.5 1.2 copy-done.1
  227.7 0.0 copy-start.3
  227.7 1.2 copy-done.3
  228.9 11.9 %finish.1 = f32[3,512,512]{2,1,0:T(8,128)} custom-call(f32[3,512,512]{2,1,0:T(8,128)} %all-reduce.2.cloned.1.call-done.sums, f32[512,512]{1,0:T(8,128)S(1)} %get-tuple-element.12.inv_one, f32[512,512]{1,0:T(8,128)S(1)} %get-tuple-element.11.inv_two, f32[512,512]{1,0:T(8,128)S(1)} %get-tuple-element.13.inv_one_t, f32[512,512]{1,0:T(8,128)S(1)} %copy-done.1, ...), custom_call_target="tpu_custom_call" | custom-call | flops 2147483648 | bytes 12582912 | tf_op jit(solution)/shard_map/finish/pallas_call | solution.py:142
  240.8 0.0 copy-done.13
Async XLA Ops:
  7.2 56.7 %all-gather.2.cloned.1.call-start = ((), (), s32[]{:S(2)}) async-start(), calls=%async_computation.1 | async-start | bytes 4456448 | tf_op jit(solution)/shard_map/all_gather | solution.py:126
  8.9 61.9 %copy-start.14 = (f32[64,512]{1,0:T(8,128)S(1)}, f32[64,512]{1,0:T(8,128)}, u32[]{:S(2)}) copy-start(f32[64,512]{1,0:T(8,128)} %param.13) | copy-start | bytes 393220
  8.9 62.0 %copy-start.15 = (f32[64,512]{1,0:T(8,128)S(1)}, f32[64,512]{1,0:T(8,128)}, u32[]{:S(2)}) copy-start(f32[64,512]{1,0:T(8,128)} %param.12) | copy-start | bytes 393220
  8.9 75.6 %copy-start.10 = (f32[64,512]{1,0:T(8,128)S(1)}, f32[64,512]{1,0:T(8,128)}, u32[]{:S(2)}) copy-start(f32[64,512]{1,0:T(8,128)} %param.10) | copy-start | bytes 393220
  9.0 74.4 %reduce-scatter.4.cloned.1.call-start = ((), (), s32[]{:S(2)}) async-start(), calls=%async_computation.3 | async-start | bytes 786432
  69.6 15.5 %copy-start.12 = (f32[64,512]{1,0:T(8,128)S(1)}, f32[64,512]{1,0:T(8,128)}, u32[]{:S(2)}) copy-start(f32[64,512]{1,0:T(8,128)} %param.11) | copy-start | bytes 393220
  70.6 155.9 %all-reduce.2.cloned.1.call-start = ((), (), s32[]{:S(2)}) async-start(), calls=%async_computation.2 | async-start | bytes 6291456 | tf_op jit(solution)/shard_map/psum | solution.py:130
  71.1 15.3 %copy-start.6 = (f32[64,512]{0,1:T(8,128)}, f32[64,512]{0,1:T(8,128)S(1)}, u32[]{:S(2)}) copy-start(f32[64,512]{0,1:T(8,128)S(1)} %copy.14) | copy-start | bytes 393220
  84.5 3.8 %copy-start.4 = (f32[64,512]{0,1:T(8,128)}, f32[64,512]{0,1:T(8,128)S(1)}, u32[]{:S(2)}) copy-start(f32[64,512]{0,1:T(8,128)S(1)} %copy.20) | copy-start | bytes 393220
  85.8 2.6 %copy-start.8 = (f32[64,512]{0,1:T(8,128)}, f32[64,512]{0,1:T(8,128)S(1)}, u32[]{:S(2)}) copy-start(f32[64,512]{0,1:T(8,128)S(1)} %copy.19) | copy-start | bytes 393220
  88.4 16.4 %copy-start.5 = (f32[64,512]{0,1:T(8,128)S(1)}, f32[64,512]{0,1:T(8,128)}, u32[]{:S(2)}) copy-start(f32[64,512]{0,1:T(8,128)} %copy-done.4) | copy-start | bytes 393220
  88.4 16.9 %copy-start.7 = (f32[64,512]{0,1:T(8,128)S(1)}, f32[64,512]{0,1:T(8,128)}, u32[]{:S(2)}) copy-start(f32[64,512]{0,1:T(8,128)} %copy-done.6) | copy-start | bytes 393220
  88.4 16.8 %copy-start.9 = (f32[64,512]{0,1:T(8,128)S(1)}, f32[64,512]{0,1:T(8,128)}, u32[]{:S(2)}) copy-start(f32[64,512]{0,1:T(8,128)} %copy-done.8) | copy-start | bytes 393220
  88.4 16.8 %copy-start.11 = (f32[512,512]{1,0:T(8,128)S(1)}, f32[512,512]{1,0:T(8,128)}, u32[]{:S(2)}) copy-start(f32[512,512]{1,0:T(8,128)} %link_ref.1) | copy-start | bytes 3145732
  102.8 1.0 copy-start
  103.7 1.1 copy-start.2
  105.3 135.6 %copy-start.13 = (f32[64,512]{1,0:T(8,128)}, f32[64,512]{1,0:T(8,128)S(1)}, u32[]{:S(2)}) copy-start(f32[64,512]{1,0:T(8,128)S(1)} %fusion.6) | copy-start | bytes 393220
  226.5 1.2 copy-start.1
  227.7 1.2 copy-start.3
Sparse Core Ops, SparseCore 0:
  10.7 53.0 all-gather.1
  70.7 12.6 reduce-scatter.3
  90.3 136.1 all-reduce.1

commit v2 on v1

v2 whole, which is shorter than its diff:
```python
import functools

import jax
import jax.numpy as jnp
from jax import lax
from jax.experimental import pallas as pl
from jax.experimental.pallas import tpu as pltpu
from jax.sharding import PartitionSpec as P

TILE = 128
BASE = 8
CORES = 2
SIDE = 2


def dot(left, right, precision=lax.Precision.HIGHEST):
    return jnp.dot(left, right, precision=precision, preferred_element_type=jnp.float32)


def high(left, right):
    return dot(left, right, lax.Precision.HIGH)


def tile_inverses(tiles):
    size = tiles[0].shape[0]
    row = lax.broadcasted_iota(jnp.int32, (size, size), 0)
    col = lax.broadcasted_iota(jnp.int32, (size, size), 1)
    eye = row == col
    one = jnp.where(eye, 1.0, 0.0)
    base = (row // BASE == col // BASE) & (row > col)
    nil, across = [], []
    for tile in tiles:
        diag = jnp.where(eye, tile, 0.0)
        down = 1.0 / jnp.sum(diag, axis=1, keepdims=True)
        across.append(1.0 / jnp.sum(diag, axis=0, keepdims=True))
        nil.append(jnp.where(base, -tile * down, 0.0))
    found = [one + n for n in nil]
    power = nil
    reach = 2
    while reach < BASE:
        power = [dot(p, p) for p in power]
        found = [f + dot(f, p) for f, p in zip(found, power)]
        reach *= 2
    found = [f * a for f, a in zip(found, across)]
    step = BASE
    while step < size:
        level = (row // (2 * step) == col // (2 * step)) & (row // step != col // step) & (row > col)
        below = [dot(jnp.where(level, t, 0.0), f) for t, f in zip(tiles, found)]
        found = [f - dot(f, b) for f, b in zip(found, below)]
        step *= 2
    return found


def place_tiles(factors, outs):
    width = factors[0].shape[0]
    count = width // TILE
    spans = [pl.ds(t * TILE, TILE) for t in range(count)]
    found = tile_inverses([f[s, s] for f in factors for s in spans])
    for i, out in enumerate(outs):
        out[...] = jnp.zeros_like(out)
        for t, s in enumerate(spans):
            out[s, s] = found[i * count + t]


def join_tiles(factors, outs):
    width = factors[0].shape[0]
    step = TILE
    while step < width:
        for at in range(0, width, 2 * step):
            top, low = pl.ds(at, step), pl.ds(at + step, step)
            belows = [dot(f[low, top], o[top, top]) for f, o in zip(factors, outs)]
            for o, b in zip(outs, belows):
                o[low, top] = -dot(o[low, low], b)
        step *= 2


def half_symmetric(x):
    row = lax.broadcasted_iota(jnp.int32, x.shape, 0)
    col = lax.broadcasted_iota(jnp.int32, x.shape, 1)
    return 0.5 * (jnp.where(row > col, x, 0.0) + jnp.where(row >= col, x, 0.0).T)


def finish(sums, inv_one, inv_two, inv_one_t, inv_two_t, mixed, mixed_t, adj_one, adj_two, out):
    sym_two = half_symmetric(adj_two[...] - sums[2])
    out[2] = high(inv_two_t[...], high(sym_two, inv_two[...]))
    turned = high(sym_two, mixed[...])
    out[1] = high(high(-inv_two_t[...], sums[1] + 2.0 * turned), inv_one[...])
    cross = high(mixed_t[...], sums[1] + turned)
    sym_one = half_symmetric(adj_one[...] - sums[0]) + 0.5 * (cross + cross.T)
    out[0] = high(inv_one_t[...], high(sym_one, inv_one[...]))


class Spread:
    def __init__(self, buf, rows, send, recv):
        self.buf, self.send, self.recv = buf, send, recv
        self.r, self.c = lax.axis_index("row"), lax.axis_index("col")
        self.depth = rows // (SIDE * CORES)
        self.z = self.r // (SIDE * CORES)
        core, side = self.r % CORES, self.r // CORES % SIDE
        self.core_peer = self.r + 1 - 2 * core
        self.side_peer = self.r + CORES - 2 * CORES * side
        self.hop = SIDE * CORES
        self.sent = []

    def copy(self, block, way, target):
        return pltpu.make_async_remote_copy(
            src_ref=self.buf.at[block],
            dst_ref=self.buf.at[block],
            send_sem=self.send.at[way, block],
            recv_sem=self.recv.at[block],
            device_id=(target, self.c),
            device_id_type=pl.DeviceIdType.MESH,
        )

    def pass_on(self, block, way, target, when):
        @pl.when(when)
        def _():
            self.copy(block, way, target).start()

        self.sent.append((block, way, target, when))

    def await_block(self, block, when):
        @pl.when(when)
        def _():
            self.copy(block, 0, self.core_peer).wait_recv()

    def begin(self):
        r, z = self.r, self.z
        self.pass_on(r, 0, r + self.hop, z < self.depth - 1)
        self.pass_on(r, 1, r - self.hop, z > 0)
        self.pass_on(r, 2, self.side_peer, z >= 0)
        self.pass_on(r, 3, self.core_peer, z >= 0)

    def origins(self, step):
        if step == 0:
            return [(0, self.z >= 0)]
        return [(-step, self.z >= step), (step, self.z < self.depth - step)]

    def along(self, step):
        z, hop = self.z, self.hop
        for away, there in self.origins(step):
            block = self.r + away * hop
            self.await_block(block, there)
            if away < 0:
                self.pass_on(block, 0, self.r + hop, there & (z < self.depth - 1))
            else:
                self.pass_on(block, 1, self.r - hop, there & (z > 0))
            self.pass_on(block, 2, self.side_peer, there)
            self.pass_on(block, 3, self.core_peer, there)

    def across(self, step):
        for away, there in self.origins(step):
            block = self.side_peer + away * self.hop
            self.await_block(block, there)
            self.pass_on(block, 3, self.core_peer, there)

    def other_core(self, step):
        for away, there in self.origins(step):
            self.await_block(self.core_peer + away * self.hop, there)
            flipped = self.side_peer + self.core_peer - self.r
            self.await_block(flipped + away * self.hop, there)

    def end(self):
        for block, way, target, when in self.sent:
            @pl.when(when)
            def _():
                self.copy(block, way, target).wait_send()


def to_peer(src, dst, send, recv, target):
    return pltpu.make_async_remote_copy(
        src_ref=src,
        dst_ref=dst,
        send_sem=send,
        recv_sem=recv,
        device_id=target,
        device_id_type=pl.DeviceIdType.MESH,
    )


def sweep(
    rows,
    cols,
    matrix,
    panel_one,
    panel_two,
    up_one,
    up_two,
    one_ref,
    two_ref,
    link_ref,
    adj_ref,
    grad_one,
    grad_two,
    sums,
    inv_one,
    inv_two,
    inv_one_t,
    inv_two_t,
    mixed,
    mixed_t,
    adj_one,
    adj_two,
    held,
    total,
    landed,
    pressed,
    outgoing,
    incoming,
    turned,
    part,
    parts,
    send_panels,
    recv_panels,
    send_carried,
    recv_carried,
    send_slices,
    recv_slices,
    send_part,
    recv_part,
    send_sums,
    recv_sums,
):
    r, c = lax.axis_index("row"), lax.axis_index("col")
    slab, width = panel_one.shape
    share = width // rows
    held[r, :, pl.ds(0, width)] = panel_one[...]
    held[r, :, pl.ds(width, width)] = panel_two[...]

    barrier = pltpu.get_barrier_semaphore()

    @pl.loop(1, rows)
    def _(i):
        pl.semaphore_signal(barrier, inc=1, device_id=(lax.rem(r + i, rows), c), device_id_type=pl.DeviceIdType.MESH)

    for i in range(1, cols):
        pl.semaphore_signal(barrier, inc=1, device_id=(r, lax.rem(c + i, cols)), device_id_type=pl.DeviceIdType.MESH)
    pl.semaphore_wait(barrier, rows + cols - 2)

    factors, inverses = (one_ref, two_ref), (inv_one, inv_two)

    def prepare_products():
        inv_one_t[...] = inv_one[...].T
        inv_two_t[...] = inv_two[...].T
        mixed[...] = high(inv_two[...], link_ref[...])
        mixed_t[...] = mixed[...].T
        adj_one[...] = high(one_ref[...].T, adj_ref[0])
        adj_two[...] = high(two_ref[...].T, adj_ref[1])

    jobs = [lambda: place_tiles(factors, inverses), lambda: join_tiles(factors, inverses), prepare_products]

    panels = Spread(held, rows, send_panels, recv_panels)
    hop = panels.hop

    def add_group(step):
        panels.other_core(step)
        for away, there in panels.origins(step):
            z = panels.z + away

            @pl.when(there)
            def _():
                columns = pl.ds(pl.multiple_of(z * (hop * slab), hop * slab), hop * slab)
                block = held[pl.ds(z * hop, hop)].reshape(hop * slab, 2 * width)
                term = -2.0 * high(matrix[:, columns], block)
                if step == 0:
                    total[...] = term
                else:
                    total[...] += term

    panels.begin()
    for step in range(1, panels.depth):
        if jobs:
            jobs.pop(0)()
        panels.along(step)
        panels.across(step - 1)
        add_group(step - 1)
    for job in jobs:
        job()
    panels.across(panels.depth - 1)
    add_group(panels.depth - 1)

    mesh_id = lambda i: lax.rem(c + i, cols)
    for i in range(1, cols):
        peer = mesh_id(i)
        to_peer(
            total.at[pl.ds(peer * slab, slab)], landed.at[c], send_carried.at[peer], recv_carried.at[c], (r, peer)
        ).start()
    carried = total[pl.ds(c * slab, slab)]
    for i in range(1, cols):
        peer = mesh_id(i)
        to_peer(
            total.at[pl.ds(peer * slab, slab)], landed.at[peer], send_carried.at[peer], recv_carried.at[peer], (r, peer)
        ).wait_recv()
        carried = carried + landed[peer]
    pressed[:, pl.ds(0, width)] = up_one[...] + carried[:, :width]
    pressed[:, pl.ds(width, width)] = up_two[...] + carried[:, width:]

    flipped_one = pressed[:, pl.ds(0, width)].T
    flipped_two = pressed[:, pl.ds(width, width)].T
    outgoing[:, pl.ds(0, share)] = flipped_one.reshape(rows, share, slab)
    outgoing[:, pl.ds(share, share)] = flipped_two.reshape(rows, share, slab)

    def slice_copy(peer, origin):
        return to_peer(
            outgoing.at[peer], incoming.at[origin], send_slices.at[peer], recv_slices.at[origin], (peer, c)
        )

    @pl.loop(1, rows)
    def _(i):
        slice_copy(lax.rem(r + i, rows), r).start()

    incoming[r] = outgoing[r]
    found_two = high(pressed[:, pl.ds(width, width)], inv_two[...])
    grad_two[...] = found_two
    grad_one[...] = high(pressed[:, pl.ds(0, width)] - high(found_two, link_ref[...]), inv_one[...])

    @pl.loop(1, rows)
    def _(i):
        peer = lax.rem(r + i, rows)
        slice_copy(peer, peer).wait_recv()

    per = TILE // slab
    for t in range(rows // per):
        turned[:, pl.ds(t * TILE, TILE)] = jnp.concatenate([incoming[t * per + i] for i in range(per)], axis=1)
    found = high(turned[...], held[...].reshape(rows * slab, 2 * width))
    part[0] = found[:share, :width]
    part[1] = found[share:, :width]
    part[2] = found[share:, width:]
    for i in range(1, cols):
        peer = mesh_id(i)
        to_peer(part, parts.at[c], send_part.at[peer], recv_part.at[c], (r, peer)).start()
    summed = part[...]
    for i in range(1, cols):
        peer = mesh_id(i)
        to_peer(part, parts.at[peer], send_part.at[peer], recv_part.at[peer], (r, peer)).wait_recv()
    for i in range(cols):
        @pl.when(c == i)
        def _():
            parts[i] = part[...]

    summed = parts[0]
    for i in range(1, cols):
        summed = summed + parts[i]
    sums[r] = summed

    whole_sums = Spread(sums, rows, send_sums, recv_sums)
    whole_sums.begin()
    for step in range(1, whole_sums.depth):
        whole_sums.along(step)
        whole_sums.across(step - 1)
    whole_sums.across(whole_sums.depth - 1)
    for step in range(whole_sums.depth):
        whole_sums.other_core(step)

    panels.end()
    whole_sums.end()
    for i in range(1, cols):
        peer = mesh_id(i)
        to_peer(
            total.at[pl.ds(peer * slab, slab)], landed.at[peer], send_carried.at[peer], recv_carried.at[peer], (r, peer)
        ).wait_send()
        to_peer(part, parts.at[peer], send_part.at[peer], recv_part.at[peer], (r, peer)).wait_send()

    @pl.loop(1, rows)
    def _(i):
        peer = lax.rem(r + i, rows)
        slice_copy(peer, peer).wait_send()


def finish_blocks(sums, *rest):
    width = sums.shape[3]
    finish([sums[:, i].reshape(width, width) for i in range(3)], *rest)


def whole(count):
    return [pl.BlockSpec(memory_space=pltpu.VMEM)] * count


def local(
    rows,
    cols,
    trail_adjoint,
    panel_one,
    panel_two,
    upstream_one,
    upstream_two,
    pivot_one,
    pivot_two,
    link_block,
    pivot_adjoint,
):
    slab, width = panel_one.shape
    share = width // rows
    matrix = trail_adjoint.reshape(trail_adjoint.shape[1], trail_adjoint.shape[3])
    float_of = lambda *shape: jax.ShapeDtypeStruct(shape, jnp.float32)
    vmem = lambda *shape: pltpu.VMEM(shape, jnp.float32)
    dma = lambda *shape: pltpu.SemaphoreType.DMA(shape)
    square = float_of(width, width)
    strip = float_of(slab, width)
    cost = pl.CostEstimate(flops=16 * width**3, bytes_accessed=48 * width**2, transcendentals=0)
    found = pl.pallas_call(
        functools.partial(sweep, rows, cols),
        out_shape=[strip, strip, float_of(rows, 3, share, width)] + [square] * 8,
        in_specs=whole(9),
        out_specs=whole(11),
        scratch_shapes=[
            vmem(rows, slab, 2 * width),
            vmem(cols * slab, 2 * width),
            vmem(cols, slab, 2 * width),
            vmem(slab, 2 * width),
            vmem(rows, 2 * share, slab),
            vmem(rows, 2 * share, slab),
            vmem(2 * share, rows * slab),
            vmem(3, share, width),
            vmem(cols, 3, share, width),
            dma(4, rows),
            dma(rows),
            dma(cols),
            dma(cols),
            dma(rows),
            dma(rows),
            dma(cols),
            dma(cols),
            dma(4, rows),
            dma(rows),
        ],
        compiler_params=pltpu.CompilerParams(
            collective_id=0, has_side_effects=True, vmem_limit_bytes=56 << 20
        ),
        cost_estimate=cost,
        name="sweep",
    )(
        matrix,
        panel_one,
        panel_two,
        upstream_one,
        upstream_two,
        pivot_one,
        pivot_two,
        link_block,
        pivot_adjoint,
    )
    grad_one, grad_two = found[:2]
    grads = pl.pallas_call(
        finish_blocks,
        out_shape=float_of(3, width, width),
        in_specs=whole(9),
        out_specs=pl.BlockSpec(memory_space=pltpu.VMEM),
        compiler_params=pltpu.CompilerParams(vmem_limit_bytes=48 << 20),
        cost_estimate=cost,
        name="finish",
    )(*found[2:])
    return grad_one, grad_two, grads


def solution(mesh):
    return jax.shard_map(
        functools.partial(local, mesh.shape["row"], mesh.shape["col"]),
        mesh=mesh,
        in_specs=(
            P("row", None, "col", None),
            P(("row", "col"), None),
            P(("row", "col"), None),
            P(("row", "col"), None),
            P(("row", "col"), None),
            P(),
            P(),
            P(),
            P(),
        ),
        out_specs=(P(("row", "col"), None), P(("row", "col"), None), P()),
        check_vma=False,
    )
```

time: 250 us -> 115 us (0.46)
  waiting for transfers between devices: 186 us -> 0 us
  Pallas kernels: 26.2 us -> 104 us
  between operations: 14 us -> 0.65 us
  matrix products: 9.94 us -> 0 us
  other arithmetic: 3.66 us -> 0 us
    psum x1 -> x0, waiting for transfers between devices: 119 us -> none  [local(): lax.psum(jnp.stack([high(pressed_one.T, panel_one), high(pressed_two.T, p...]
    pallas_call x2, Pallas kernels: 26.2 us -> 104 us  [the longest x1 92.5 us: local(): pl.pallas_call(functools.partial(sweep, rows, cols), out_shape=[strip, st...]
    all_gather x1 -> x0, waiting for transfers between devices: 54.8 us -> none  [local(): summed = high(matrix, lax.all_gather(stacked, 'row', axis=0, tiled=True))]
    unnamed x4 -> x0, waiting for transfers between devices: 12.3 us -> none
    dot_general x7 -> x0, matrix products: 9.94 us -> none  [dot(): jnp.dot(left, right, precision=precision, preferred_element_type=jnp.floa...]
    unnamed x37 -> x17, local copies, waits for them, and re-layouts: 6.03 us -> 9.36 us
  transfers between devices with their start and end apart: 3 -> 0, of which waited for: 3 -> 0; matrix products, arithmetic and copies ran while one was open for 1% -> 0% of each run, Pallas kernels for 6% -> 0%
where the time goes in v2:
time: 115 us; the launch traced here: 114 us
  Pallas kernels  104 us (90%)
  local copies, waits for them, and re-layouts  9.36 us (8%)
    pallas_call x1, Pallas kernels, local(): pl.pallas_call(functools.partial(sweep, rows, cols), out_shape=[strip, st...  92.5 us
    pallas_call x1, Pallas kernels, local(): pl.pallas_call(finish_blocks, out_shape=float_of(3, width, width), in_spe...  11.9 us
    unnamed x17, local copies, waits for them, and re-layouts  9.36 us

profile of v2, /device:TPU:1, one launch (start us, length us, event | category | flops | bytes accessed | tf_op | source)
XLA Modules:
  0.0 114.5 jit_solution(387087518360186754)
XLA Ops:
  0.6 1.9 %copy.14 = f32[1,128,1,1024]{3,1,2,0:T(8,128)} copy(f32[1,128,1,1024]{3,2,1,0:T(1,128)} %param.9) | data formatting | bytes 1048576
  2.6 92.5 %sweep.1 = (f32[64,512]{1,0:T(8,128)}, f32[64,512]{1,0:T(8,128)}, f32[16,3,32,512]{3,2,1,0:T(8,128)}, f32[512,512]{1,0:T(8,128)}, f32[512,512]{1,0:T(8,128)}, /*...) custom-call(f32[128,1024]{1,0:T(8,128)} %bitcast.3, ...), custom_call_target="tpu_custom_call" | custom-call | flops 2147483648 | bytes 12582912 | tf_op jit(solution)/shard_map/sweep/pallas_call | solution.py:401
  95.1 0.0 copy-start
  95.1 1.2 %copy-done = f32[512,512]{1,0:T(8,128)S(1)} copy-done((f32[512,512]{1,0:T(8,128)S(1)}, f32[512,512]{1,0:T(8,128)}, u32[]{:S(2)}) %copy-start) | copy-done | bytes 1048600
  96.3 0.0 copy-start.1
  96.3 1.2 %copy-done.1 = f32[512,512]{1,0:T(8,128)S(1)} copy-done((f32[512,512]{1,0:T(8,128)S(1)}, f32[512,512]{1,0:T(8,128)}, u32[]{:S(2)}) %copy-start.1) | copy-done | bytes 1048600
  97.6 0.0 copy-start.2
  97.6 1.2 %copy-done.2 = f32[512,512]{1,0:T(8,128)S(1)} copy-done((f32[512,512]{1,0:T(8,128)S(1)}, f32[512,512]{1,0:T(8,128)}, u32[]{:S(2)}) %copy-start.2) | copy-done | bytes 1048600
  98.8 0.0 copy-start.3
  98.8 1.2 %copy-done.3 = f32[512,512]{1,0:T(8,128)S(1)} copy-done((f32[512,512]{1,0:T(8,128)S(1)}, f32[512,512]{1,0:T(8,128)}, u32[]{:S(2)}) %copy-start.3) | copy-done | bytes 1048600
  100.0 0.0 copy-start.4
  100.0 1.2 %copy-done.4 = f32[512,512]{1,0:T(8,128)S(1)} copy-done((f32[512,512]{1,0:T(8,128)S(1)}, f32[512,512]{1,0:T(8,128)}, u32[]{:S(2)}) %copy-start.4) | copy-done | bytes 1048600
  101.2 0.0 copy-start.6
  101.2 0.0 copy-start.5
  101.2 11.9 %finish.1 = f32[3,512,512]{2,1,0:T(8,128)} custom-call(f32[16,3,32,512]{3,2,1,0:T(8,128)} %get-tuple-element.16.sums, f32[512,512]{1,0:T(8,128)S(1)} %copy-done, f32[512,512]{1,0:T(8,128)S(1)} %copy-done.1, f32[512,512]{1,0:T(8,128)S(1)} %copy-done.2, f32[512,512]{1,0:T(8,128)S(1)} %copy-done.3, f32[512,512]{1,0:T(8,128)S(1)} %copy-done.4, ...), custom_call_target="tpu_custom_call" | custom-call | flops 2147483648 | bytes 12582912 | tf_op jit(solution)/shard_map/finish/pallas_call | solution.py:444
  113.2 0.0 copy-done.6
  113.2 0.7 copy.17
  113.8 0.0 copy-done.5
  113.8 0.7 copy.18
Async XLA Ops:
  95.1 1.2 %copy-start = (f32[512,512]{1,0:T(8,128)S(1)}, f32[512,512]{1,0:T(8,128)}, u32[]{:S(2)}) copy-start(f32[512,512]{1,0:T(8,128)} %get-tuple-element.17.rest_0_) | copy-start | bytes 3145732
  96.3 1.2 %copy-start.1 = (f32[512,512]{1,0:T(8,128)S(1)}, f32[512,512]{1,0:T(8,128)}, u32[]{:S(2)}) copy-start(f32[512,512]{1,0:T(8,128)} %get-tuple-element.18.rest_1_) | copy-start | bytes 3145732
  97.6 1.2 %copy-start.2 = (f32[512,512]{1,0:T(8,128)S(1)}, f32[512,512]{1,0:T(8,128)}, u32[]{:S(2)}) copy-start(f32[512,512]{1,0:T(8,128)} %get-tuple-element.19.rest_2_) | copy-start | bytes 3145732
  98.8 1.2 %copy-start.3 = (f32[512,512]{1,0:T(8,128)S(1)}, f32[512,512]{1,0:T(8,128)}, u32[]{:S(2)}) copy-start(f32[512,512]{1,0:T(8,128)} %get-tuple-element.20.rest_3_) | copy-start | bytes 3145732
  100.0 1.2 %copy-start.4 = (f32[512,512]{1,0:T(8,128)S(1)}, f32[512,512]{1,0:T(8,128)}, u32[]{:S(2)}) copy-start(f32[512,512]{1,0:T(8,128)} %get-tuple-element.21.rest_4_) | copy-start | bytes 3145732
  101.2 11.9 %copy-start.6 = (f32[64,512]{1,0:T(8,128)S(1)}, f32[64,512]{1,0:T(8,128)}, u32[]{:S(2)}) copy-start(f32[64,512]{1,0:T(8,128)} %get-tuple-element.28) | copy-start | bytes 393220
  101.2 12.6 %copy-start.5 = (f32[64,512]{1,0:T(8,128)S(1)}, f32[64,512]{1,0:T(8,128)}, u32[]{:S(2)}) copy-start(f32[64,512]{1,0:T(8,128)} %get-tuple-element.29) | copy-start | bytes 393220

commit v3 on v2

--- a/solution.py
+++ b/solution.py
@@ -80,14 +80,31 @@
     return 0.5 * (jnp.where(row > col, x, 0.0) + jnp.where(row >= col, x, 0.0).T)
 
 
-def finish(sums, inv_one, inv_two, inv_one_t, inv_two_t, mixed, mixed_t, adj_one, adj_two, out):
-    sym_two = half_symmetric(adj_two[...] - sums[2])
-    out[2] = high(inv_two_t[...], high(sym_two, inv_two[...]))
+def times_lower(left, lower):
+    half = lower.shape[0] // 2
+    return jnp.concatenate(
+        [high(left, lower[:, pl.ds(0, half)]), high(left[:, half:], lower[pl.ds(half, half), pl.ds(half, half)])],
+        axis=1,
+    )
+
+
+def upper_times(upper, right):
+    half = upper.shape[0] // 2
+    return jnp.concatenate(
+        [high(upper[pl.ds(0, half)], right), high(upper[pl.ds(half, half), pl.ds(half, half)], right[half:])],
+        axis=0,
+    )
+
+
+def finish(sum_one, sum_link, sum_two, inv_one, inv_two, inv_one_t, inv_two_t, mixed, mixed_t, adj_one, adj_two, out):
+    sym_two = half_symmetric(adj_two[...] - sum_two[...])
+    out[2] = upper_times(inv_two_t, times_lower(sym_two, inv_two))
     turned = high(sym_two, mixed[...])
-    out[1] = high(high(-inv_two_t[...], sums[1] + 2.0 * turned), inv_one[...])
-    cross = high(mixed_t[...], sums[1] + turned)
-    sym_one = half_symmetric(adj_one[...] - sums[0]) + 0.5 * (cross + cross.T)
-    out[0] = high(inv_one_t[...], high(sym_one, inv_one[...]))
+    link = sum_link[...]
+    out[1] = -times_lower(upper_times(inv_two_t, link + 2.0 * turned), inv_one)
+    cross = high(mixed_t[...], link + turned)
+    sym_one = half_symmetric(adj_one[...] - sum_one[...]) + 0.5 * (cross + cross.T)
+    out[0] = upper_times(inv_one_t, times_lower(sym_one, inv_one))
 
 
 class Spread:
@@ -181,18 +198,30 @@
 def sweep(
     rows,
     cols,
-    matrix,
+    matrix_in,
     panel_one,
     panel_two,
+    up_one_in,
+    up_two_in,
+    one_in,
+    two_in,
+    link_in,
+    adj_in,
+    grad_one,
+    grad_two,
+    grads,
+    matrix,
     up_one,
     up_two,
     one_ref,
     two_ref,
     link_ref,
     adj_ref,
-    grad_one,
-    grad_two,
+    read_sem,
     sums,
+    sum_one,
+    sum_link,
+    sum_two,
     inv_one,
     inv_two,
     inv_one_t,
@@ -224,6 +253,20 @@
     r, c = lax.axis_index("row"), lax.axis_index("col")
     slab, width = panel_one.shape
     share = width // rows
+    reads = [
+        pltpu.make_async_copy(source, target, read_sem.at[i])
+        for i, (source, target) in enumerate(
+            [
+                (one_in, one_ref),
+                (two_in, two_ref),
+                (link_in, link_ref),
+                (adj_in, adj_ref),
+                (matrix_in.at[0, :, 0], matrix),
+                (up_one_in, up_one),
+                (up_two_in, up_two),
+            ]
+        )
+    ]
     held[r, :, pl.ds(0, width)] = panel_one[...]
     held[r, :, pl.ds(width, width)] = panel_two[...]
 
@@ -268,6 +311,10 @@
                     total[...] += term
 
     panels.begin()
+    for read in reads:
+        read.start()
+    for read in reads:
+        read.wait()
     for step in range(1, panels.depth):
         if jobs:
             jobs.pop(0)()
@@ -297,8 +344,11 @@
 
     flipped_one = pressed[:, pl.ds(0, width)].T
     flipped_two = pressed[:, pl.ds(width, width)].T
-    outgoing[:, pl.ds(0, share)] = flipped_one.reshape(rows, share, slab)
-    outgoing[:, pl.ds(share, share)] = flipped_two.reshape(rows, share, slab)
+    for i in range(rows):
+        mirror = rows - 1 - i
+        outgoing[i] = jnp.concatenate(
+            [flipped_one[i * share : (i + 1) * share], flipped_two[mirror * share : (mirror + 1) * share]], axis=1
+        )
 
     def slice_copy(peer, origin):
         return to_peer(
@@ -321,23 +371,27 @@
 
     per = TILE // slab
     for t in range(rows // per):
-        turned[:, pl.ds(t * TILE, TILE)] = jnp.concatenate([incoming[t * per + i] for i in range(per)], axis=1)
+        pieces = [incoming[t * per + i] for i in range(per)]
+        turned[pl.ds(0, share), pl.ds(t * TILE, TILE)] = jnp.concatenate([p[:, :slab] for p in pieces], axis=1)
+        turned[pl.ds(share, share), pl.ds(t * TILE, TILE)] = jnp.concatenate([p[:, slab:] for p in pieces], axis=1)
     found = high(turned[...], held[...].reshape(rows * slab, 2 * width))
-    part[0] = found[:share, :width]
-    part[1] = found[share:, :width]
-    part[2] = found[share:, width:]
+    part[:, pl.ds(0, width)] = found[share:, :width]
+    levels = width // TILE
+    for level in range(levels):
+
+        @pl.when(r * share // TILE == level)
+        def _():
+            reach = (level + 1) * TILE
+            part[:, pl.ds(width, reach)] = found[:share, :reach]
+            part[:, pl.ds(width + reach, width + TILE - reach)] = found[share:, width : 2 * width + TILE - reach]
+
     for i in range(1, cols):
         peer = mesh_id(i)
         to_peer(part, parts.at[c], send_part.at[peer], recv_part.at[c], (r, peer)).start()
-    summed = part[...]
+    parts[c] = part[...]
     for i in range(1, cols):
         peer = mesh_id(i)
         to_peer(part, parts.at[peer], send_part.at[peer], recv_part.at[peer], (r, peer)).wait_recv()
-    for i in range(cols):
-        @pl.when(c == i)
-        def _():
-            parts[i] = part[...]
-
     summed = parts[0]
     for i in range(1, cols):
         summed = summed + parts[i]
@@ -351,6 +405,17 @@
     whole_sums.across(whole_sums.depth - 1)
     for step in range(whole_sums.depth):
         whole_sums.other_core(step)
+    sum_one[...] = jnp.zeros_like(sum_one)
+    sum_two[...] = jnp.zeros_like(sum_two)
+    for i in range(rows):
+        reach = (i * share // TILE + 1) * TILE
+        own, mirror = pl.ds(i * share, share), pl.ds((rows - 1 - i) * share, share)
+        sum_link[mirror] = sums[i, :, pl.ds(0, width)]
+        sum_one[own, pl.ds(0, reach)] = sums[i, :, pl.ds(width, reach)]
+        sum_two[mirror, pl.ds(0, width + TILE - reach)] = sums[i, :, pl.ds(width + reach, width + TILE - reach)]
+    finish(
+        sum_one, sum_link, sum_two, inv_one, inv_two, inv_one_t, inv_two_t, mixed, mixed_t, adj_one, adj_two, grads
+    )
 
     panels.end()
     whole_sums.end()
@@ -365,11 +430,6 @@
     def _(i):
         peer = lax.rem(r + i, rows)
         slice_copy(peer, peer).wait_send()
-
-
-def finish_blocks(sums, *rest):
-    width = sums.shape[3]
-    finish([sums[:, i].reshape(width, width) for i in range(3)], *rest)
 
 
 def whole(count):
@@ -391,28 +451,40 @@
 ):
     slab, width = panel_one.shape
     share = width // rows
-    matrix = trail_adjoint.reshape(trail_adjoint.shape[1], trail_adjoint.shape[3])
     float_of = lambda *shape: jax.ShapeDtypeStruct(shape, jnp.float32)
     vmem = lambda *shape: pltpu.VMEM(shape, jnp.float32)
     dma = lambda *shape: pltpu.SemaphoreType.DMA(shape)
-    square = float_of(width, width)
+    square = vmem(width, width)
     strip = float_of(slab, width)
     cost = pl.CostEstimate(flops=16 * width**3, bytes_accessed=48 * width**2, transcendentals=0)
-    found = pl.pallas_call(
+    packed = 2 * width + TILE
+    return pl.pallas_call(
         functools.partial(sweep, rows, cols),
-        out_shape=[strip, strip, float_of(rows, 3, share, width)] + [square] * 8,
-        in_specs=whole(9),
-        out_specs=whole(11),
+        out_shape=[strip, strip, float_of(3, width, width)],
+        in_specs=[pl.BlockSpec(memory_space=pl.ANY)] + whole(2) + [pl.BlockSpec(memory_space=pl.ANY)] * 6,
+        out_specs=whole(3),
         scratch_shapes=[
+            vmem(cols * slab, rows * slab),
+            vmem(slab, width),
+            vmem(slab, width),
+            square,
+            square,
+            square,
+            vmem(2, width, width),
+            dma(7),
+            vmem(rows, share, packed),
+        ]
+        + [square] * 11
+        + [
             vmem(rows, slab, 2 * width),
             vmem(cols * slab, 2 * width),
             vmem(cols, slab, 2 * width),
             vmem(slab, 2 * width),
-            vmem(rows, 2 * share, slab),
-            vmem(rows, 2 * share, slab),
+            vmem(rows, share, 2 * slab),
+            vmem(rows, share, 2 * slab),
             vmem(2 * share, rows * slab),
-            vmem(3, share, width),
-            vmem(cols, 3, share, width),
+            vmem(share, packed),
+            vmem(cols, share, packed),
             dma(4, rows),
             dma(rows),
             dma(cols),
@@ -430,7 +502,7 @@
         cost_estimate=cost,
         name="sweep",
     )(
-        matrix,
+        trail_adjoint,
         panel_one,
         panel_two,
         upstream_one,
@@ -440,17 +512,6 @@
         link_block,
         pivot_adjoint,
     )
-    grad_one, grad_two = found[:2]
-    grads = pl.pallas_call(
-        finish_blocks,
-        out_shape=float_of(3, width, width),
-        in_specs=whole(9),
-        out_specs=pl.BlockSpec(memory_space=pltpu.VMEM),
-        compiler_params=pltpu.CompilerParams(vmem_limit_bytes=48 << 20),
-        cost_estimate=cost,
-        name="finish",
-    )(*found[2:])
-    return grad_one, grad_two, grads
 
 
 def solution(mesh):

time: 115 us -> 94.3 us (0.82)
  Pallas kernels: 104 us -> 86.5 us
  local copies, waits for them, and re-layouts: 9.36 us -> 6.99 us
    pallas_call x1 -> x0, Pallas kernels: 11.9 us -> none  [local(): pl.pallas_call(finish_blocks, out_shape=float_of(3, width, width), in_spe...]
    pallas_call x1, Pallas kernels: 92.5 us -> 86.5 us  [local(): pl.pallas_call(functools.partial(sweep, rows, cols), out_shape=[strip, st...]
    unnamed x17 -> x3, local copies, waits for them, and re-layouts: 9.36 us -> 6.99 us
where the time goes in v3:
time: 94.3 us; the launch traced here: 94.1 us
  Pallas kernels  86.5 us (92%)
  local copies, waits for them, and re-layouts  6.99 us (7%)
    pallas_call x1, Pallas kernels, local(): pl.pallas_call(functools.partial(sweep, rows, cols), out_shape=[strip, st...  86.5 us
    unnamed x3, local copies, waits for them, and re-layouts  6.99 us

profile of v3, /device:TPU:1, one launch (start us, length us, event | category | flops | bytes accessed | tf_op | source)
XLA Modules:
  0.0 94.1 jit_solution(18173426715998746421)
XLA Ops:
  0.6 86.5 %sweep.1 = (f32[64,512]{1,0:T(8,128)}, f32[64,512]{1,0:T(8,128)}, f32[3,512,512]{2,1,0:T(8,128)}) custom-call(f32[1,128,1,1024]{3,2,1,0:T(1,128)} %matrix_in.1, f32[64,512]{1,0:T(8,128)} %panel_one.1, f32[64,512]{1,0:T(8,128)} %panel_two.1, f32[64,512]{1,0:T(8,128)} %up_one_in.1, f32[64,512]{1,0:T(8,128)} %up_two_in.1, f32[512,512]{1,0:T(8,128)} %one_in.1, ...), custom_call_target="tpu_custom_call" | custom-call | flops 2147483648 | bytes 12582912 | tf_op jit(solution)/shard_map/sweep/pallas_call | solution.py:461
  87.1 1.6 %copy.15 = f32[64,512]{1,0:T(8,128)} copy(f32[64,512]{1,0:T(8,128)} %get-tuple-element.6) | data formatting | bytes 262144
  88.7 1.6 %copy.16 = f32[64,512]{1,0:T(8,128)} copy(f32[64,512]{1,0:T(8,128)} %get-tuple-element.7) | data formatting | bytes 262144
  90.2 3.9 %copy.17 = f32[3,512,512]{2,1,0:T(8,128)} copy(f32[3,512,512]{2,1,0:T(8,128)} %get-tuple-element.8) | data formatting | bytes 6291456

commit v4 on v3

--- a/solution.py
+++ b/solution.py
@@ -21,10 +21,12 @@
     return dot(left, right, lax.Precision.HIGH)
 
 
-def tile_inverses(tiles):
-    size = tiles[0].shape[0]
-    row = lax.broadcasted_iota(jnp.int32, (size, size), 0)
-    col = lax.broadcasted_iota(jnp.int32, (size, size), 1)
+def tile_grid(size):
+    return lax.broadcasted_iota(jnp.int32, (size, size), 0), lax.broadcasted_iota(jnp.int32, (size, size), 1)
+
+
+def base_inverses(tiles):
+    row, col = tile_grid(tiles[0].shape[0])
     eye = row == col
     one = jnp.where(eye, 1.0, 0.0)
     base = (row // BASE == col // BASE) & (row > col)
@@ -41,9 +43,12 @@
         power = [dot(p, p) for p in power]
         found = [f + dot(f, p) for f, p in zip(found, power)]
         reach *= 2
-    found = [f * a for f, a in zip(found, across)]
-    step = BASE
-    while step < size:
+    return [f * a for f, a in zip(found, across)]
+
+
+def raise_inverses(tiles, found, step, last):
+    row, col = tile_grid(tiles[0].shape[0])
+    while step < last:
         level = (row // (2 * step) == col // (2 * step)) & (row // step != col // step) & (row > col)
         below = [dot(jnp.where(level, t, 0.0), f) for t, f in zip(tiles, found)]
         found = [f - dot(f, b) for f, b in zip(found, below)]
@@ -51,15 +56,25 @@
     return found
 
 
-def place_tiles(factors, outs):
-    width = factors[0].shape[0]
-    count = width // TILE
-    spans = [pl.ds(t * TILE, TILE) for t in range(count)]
-    found = tile_inverses([f[s, s] for f in factors for s in spans])
-    for i, out in enumerate(outs):
+def tile_spans(factors):
+    spans = [pl.ds(t * TILE, TILE) for t in range(factors[0].shape[0] // TILE)]
+    return [(i, s) for i in range(len(factors)) for s in spans]
+
+
+def place_bases(factors, outs):
+    spans = tile_spans(factors)
+    found = base_inverses([factors[i][s, s] for i, s in spans])
+    for out in outs:
         out[...] = jnp.zeros_like(out)
-        for t, s in enumerate(spans):
-            out[s, s] = found[i * count + t]
+    for (i, s), f in zip(spans, found):
+        outs[i][s, s] = f
+
+
+def raise_tiles(factors, outs, step, last):
+    spans = tile_spans(factors)
+    found = raise_inverses([factors[i][s, s] for i, s in spans], [outs[i][s, s] for i, s in spans], step, last)
+    for (i, s), f in zip(spans, found):
+        outs[i][s, s] = f
 
 
 def join_tiles(factors, outs):
@@ -96,15 +111,18 @@
     )
 
 
-def finish(sum_one, sum_link, sum_two, inv_one, inv_two, inv_one_t, inv_two_t, mixed, mixed_t, adj_one, adj_two, out):
+def finish(sum_one, sum_link, sum_two, inv_one, inv_two, inv_one_t, inv_two_t, mixed, mixed_t, adj_one, adj_two, out, writes):
     sym_two = half_symmetric(adj_two[...] - sum_two[...])
     out[2] = upper_times(inv_two_t, times_lower(sym_two, inv_two))
+    writes[2].start()
     turned = high(sym_two, mixed[...])
     link = sum_link[...]
     out[1] = -times_lower(upper_times(inv_two_t, link + 2.0 * turned), inv_one)
+    writes[1].start()
     cross = high(mixed_t[...], link + turned)
     sym_one = half_symmetric(adj_one[...] - sum_one[...]) + 0.5 * (cross + cross.T)
     out[0] = upper_times(inv_one_t, times_lower(sym_one, inv_one))
+    writes[0].start()
 
 
 class Spread:
@@ -207,9 +225,13 @@
     two_in,
     link_in,
     adj_in,
+    grad_one_out,
+    grad_two_out,
+    grads_out,
     grad_one,
     grad_two,
     grads,
+    write_sem,
     matrix,
     up_one,
     up_two,
@@ -259,9 +281,9 @@
             [
                 (one_in, one_ref),
                 (two_in, two_ref),
+                (matrix_in.at[0, :, 0], matrix),
                 (link_in, link_ref),
                 (adj_in, adj_ref),
-                (matrix_in.at[0, :, 0], matrix),
                 (up_one_in, up_one),
                 (up_two_in, up_two),
             ]
@@ -282,15 +304,28 @@
 
     factors, inverses = (one_ref, two_ref), (inv_one, inv_two)
 
-    def prepare_products():
+    def first_job():
+        for read in reads[:3]:
+            read.wait()
+        place_bases(factors, inverses)
+
+    def second_job():
+        raise_tiles(factors, inverses, BASE, TILE)
+        for read in reads[3:]:
+            read.wait()
+
+    def third_job():
+        join_tiles(factors, inverses)
         inv_one_t[...] = inv_one[...].T
         inv_two_t[...] = inv_two[...].T
+
+    def fourth_job():
         mixed[...] = high(inv_two[...], link_ref[...])
         mixed_t[...] = mixed[...].T
         adj_one[...] = high(one_ref[...].T, adj_ref[0])
         adj_two[...] = high(two_ref[...].T, adj_ref[1])
 
-    jobs = [lambda: place_tiles(factors, inverses), lambda: join_tiles(factors, inverses), prepare_products]
+    jobs = [first_job, second_job, third_job, fourth_job]
 
     panels = Spread(held, rows, send_panels, recv_panels)
     hop = panels.hop
@@ -313,8 +348,6 @@
     panels.begin()
     for read in reads:
         read.start()
-    for read in reads:
-        read.wait()
     for step in range(1, panels.depth):
         if jobs:
             jobs.pop(0)()
@@ -359,10 +392,18 @@
     def _(i):
         slice_copy(lax.rem(r + i, rows), r).start()
 
+    writes = [
+        pltpu.make_async_copy(source, target, write_sem.at[i])
+        for i, (source, target) in enumerate(
+            [(grads.at[k], grads_out.at[k]) for k in range(3)] + [(grad_one, grad_one_out), (grad_two, grad_two_out)]
+        )
+    ]
     incoming[r] = outgoing[r]
     found_two = high(pressed[:, pl.ds(width, width)], inv_two[...])
     grad_two[...] = found_two
     grad_one[...] = high(pressed[:, pl.ds(0, width)] - high(found_two, link_ref[...]), inv_one[...])
+    writes[3].start()
+    writes[4].start()
 
     @pl.loop(1, rows)
     def _(i):
@@ -414,7 +455,19 @@
         sum_one[own, pl.ds(0, reach)] = sums[i, :, pl.ds(width, reach)]
         sum_two[mirror, pl.ds(0, width + TILE - reach)] = sums[i, :, pl.ds(width + reach, width + TILE - reach)]
     finish(
-        sum_one, sum_link, sum_two, inv_one, inv_two, inv_one_t, inv_two_t, mixed, mixed_t, adj_one, adj_two, grads
+        sum_one,
+        sum_link,
+        sum_two,
+        inv_one,
+        inv_two,
+        inv_one_t,
+        inv_two_t,
+        mixed,
+        mixed_t,
+        adj_one,
+        adj_two,
+        grads,
+        writes,
     )
 
     panels.end()
@@ -430,6 +483,25 @@
     def _(i):
         peer = lax.rem(r + i, rows)
         slice_copy(peer, peer).wait_send()
+
+    for write in writes:
+        write.wait()
+
+
+def hand_on(*refs):
+    *ends, sem = refs
+    count = len(ends) // 2
+    pairs = []
+    for source, target in zip(ends[:count], ends[count:]):
+        if len(source.shape) == 3:
+            pairs += [(source.at[k], target.at[k]) for k in range(source.shape[0])]
+        else:
+            pairs.append((source, target))
+    copies = [pltpu.make_async_copy(source, target, sem.at[i]) for i, (source, target) in enumerate(pairs)]
+    for copy in copies:
+        copy.start()
+    for copy in copies:
+        copy.wait()
 
 
 def whole(count):
@@ -458,12 +530,18 @@
     strip = float_of(slab, width)
     cost = pl.CostEstimate(flops=16 * width**3, bytes_accessed=48 * width**2, transcendentals=0)
     packed = 2 * width + TILE
-    return pl.pallas_call(
+    results = [strip, strip, float_of(3, width, width)]
+    anywhere = lambda count: [pl.BlockSpec(memory_space=pl.ANY)] * count
+    found = pl.pallas_call(
         functools.partial(sweep, rows, cols),
-        out_shape=[strip, strip, float_of(3, width, width)],
-        in_specs=[pl.BlockSpec(memory_space=pl.ANY)] + whole(2) + [pl.BlockSpec(memory_space=pl.ANY)] * 6,
-        out_specs=whole(3),
+        out_shape=results,
+        in_specs=anywhere(1) + whole(2) + anywhere(6),
+        out_specs=anywhere(3),
         scratch_shapes=[
+            vmem(slab, width),
+            vmem(slab, width),
+            vmem(3, width, width),
+            dma(5),
             vmem(cols * slab, rows * slab),
             vmem(slab, width),
             vmem(slab, width),
@@ -512,6 +590,15 @@
         link_block,
         pivot_adjoint,
     )
+    return pl.pallas_call(
+        hand_on,
+        out_shape=results,
+        in_specs=anywhere(3),
+        out_specs=anywhere(3),
+        scratch_shapes=[dma(5)],
+        compiler_params=pltpu.CompilerParams(vmem_limit_bytes=56 << 20),
+        name="hand_on",
+    )(*found)
 
 
 def solution(mesh):

time: 94.3 us -> 193 us (2.05)
  Pallas kernels: 86.5 us -> 192 us
  local copies, waits for them, and re-layouts: 6.99 us -> 0 us
    pallas_call x1 -> x2, Pallas kernels: 86.5 us -> 192 us  [the longest x1 104 us: local(): pl.pallas_call(hand_on, out_shape=results, in_specs=anywhere(3), out_spec...]
    unnamed x3 -> x0, local copies, waits for them, and re-layouts: 6.99 us -> none
where the time goes in v4:
time: 193 us
  Pallas kernels  192 us (99%)
    pallas_call x1, Pallas kernels, local(): pl.pallas_call(hand_on, out_shape=results, in_specs=anywhere(3), out_spec...  104 us
    pallas_call x1, Pallas kernels, local(): pl.pallas_call(functools.partial(sweep, rows, cols), out_shape=results, i...  87.3 us

profile of v4, /device:TPU:1, one launch (start us, length us, event | category | flops | bytes accessed | tf_op | source)
XLA Modules:
  0.0 192.5 jit_solution(13469345734107428976)
XLA Ops:
  0.6 87.3 %sweep.1 = (f32[64,512]{1,0:T(8,128)}, f32[64,512]{1,0:T(8,128)}, f32[3,512,512]{2,1,0:T(8,128)}) custom-call(f32[1,128,1,1024]{3,2,1,0:T(1,128)} %matrix_in.1, f32[64,512]{1,0:T(8,128)} %panel_one.1, f32[64,512]{1,0:T(8,128)} %panel_two.1, f32[64,512]{1,0:T(8,128)} %up_one_in.1, f32[64,512]{1,0:T(8,128)} %up_two_in.1, f32[512,512]{1,0:T(8,128)} %one_in.1, ...), custom_call_target="tpu_custom_call" | custom-call | flops 2147483648 | bytes 12582912 | tf_op jit(solution)/shard_map/sweep/pallas_call | solution.py:535
  88.0 104.4 %hand_on.1 = (f32[64,512]{1,0:T(8,128)}, f32[64,512]{1,0:T(8,128)}, f32[3,512,512]{2,1,0:T(8,128)}) custom-call(f32[64,512]{1,0:T(8,128)} %get-tuple-element.6.refs_0_, f32[64,512]{1,0:T(8,128)} %get-tuple-element.7.refs_1_, f32[3,512,512]{2,1,0:T(8,128)} %get-tuple-element.8.refs_2_), custom_call_target="tpu_custom_call" | custom-call | tf_op jit(solution)/shard_map/hand_on/pallas_call | solution.py:593
